TPU v7x, 32 devices: a whole 2x2x4 slice. The times are simulated.
32 devices in a mesh: groups: 2 (over y), serial: 4 (over z), level: 2 (over x), feat: 2 (over core).
Axes of the slice: x: 2, y: 2, z: 4, core: 2. Of those that a mesh axis runs over, the one named last changes fastest.
Arguments:
- points: bfloat16 [65536, 64], P(('groups', 'serial', 'level')), parts along dimension 0, may hold values from -6 to 6
- patch_ids: int32 [65536], P(('groups', 'serial', 'level')), parts along dimension 0, may hold values from 0 to 63, never falling along the last dimension, each value on 1 to 1024 neighbouring positions
- child_counts: int32 [16, 2048], P(('groups', 'serial', 'level')), parts along dimension 0, may hold values from 1 to 8, 4096 in all within a row
- voxel_slot: int32 [32768], P(('groups', 'serial', 'level')), parts along dimension 0, may hold values from 0 to 16383, as said below
- w_query0: bfloat16 [64, 64], P(None, 'feat'), may hold values from -2 to 2
- w_key0: bfloat16 [64, 64], P(None, 'feat'), may hold values from -2 to 2
- w_value0: bfloat16 [64, 64], P(None, 'feat'), may hold values from -6 to 6
- w_attn_out0: bfloat16 [64, 64], P('feat'), may hold values from -3 to 3
- w_mlp_in: bfloat16 [64, 256], P(None, 'feat'), may hold values from -0.75 to 0.75
- w_mlp_out: bfloat16 [256, 64], P('feat'), may hold values from -0.375 to 0.375
- w_pool: bfloat16 [64, 128], replicated, may hold values from -0.75 to 0.75
- w_query1: bfloat16 [128, 128], P(None, 'feat'), may hold values from -2 to 2
- w_key1: bfloat16 [128, 128], P(None, 'feat'), may hold values from -2 to 2
- w_value1: bfloat16 [128, 128], P(None, 'feat'), may hold values from -0.5 to 0.5
- w_attn_out1: bfloat16 [128, 128], P('feat'), may hold values from -0.5 to 0.5
- w_up: bfloat16 [128, 64], replicated, may hold values from -0.5 to 0.5
Outputs:
- refined: bfloat16 [65536, 64], P(('groups', 'serial', 'level')), parts along dimension 0
There are 2 independent parts, one for each index of `groups`. A program takes and returns all parts, laid end to end along the dimension named above; an argument that names none is the same for every part. Nothing has to cross between parts.
Inputs may be any that keep to these rules, and one draw needn't show every extreme that they name: `patch_ids`: never falls along the points; each patch is a run of consecutive points. `child_counts`: each row sums to 4096. `voxel_slot`: A permutation of 0 to 16383. Position g belongs to shard g // 2048 (shard s * 2 + l has serial index s and level index l); a voxel goes to a shard of the same level index as its own shard; from one shard to one shard go at most 1024 voxels, and that many in some pair of every level index.
All inputs are finite; a program needn't handle non-finite values.
Results may differ from a plain program's by a relative error of at most 0.005.
The roundings to bfloat16 on the way count: a program that leaves them out, or rounds other values in their place, can miss the bound.
Values may be sent and summed in bfloat16 or wider, within the bound.
A program may use at most 64 MiB of HBM per device.

v0:
```python
import functools

import jax
import jax.numpy as jnp
from jax import lax
from jax.experimental import pallas as pl
from jax.experimental.pallas import tpu as pltpu
from jax.sharding import PartitionSpec as P

HEAD = 16
PATCH = 1024
EPSILON = 1e-05
NEG_LARGE = -1e30
TILE = 256
SPAN = 384
HI_ROWS = 64
LO_ROWS = 128
OUTSIDE = 1 << 20
MESH = pl.DeviceIdType.MESH
BF16 = jnp.bfloat16
F32 = jnp.float32
VMEM = pl.BlockSpec(memory_space=pltpu.VMEM)
SMEM = pl.BlockSpec(memory_space=pltpu.SMEM)
VMEM_BYTES = 50 * 1024 * 1024

NN = (((1,), (0,)), ((), ()))
NT = (((1,), (1,)), ((), ()))
TN = (((0,), (0,)), ((), ()))


def dot(a, b, dims=NN):
    return lax.dot_general(a, b, dims, preferred_element_type=F32)


def norm(values):
    values = values.astype(F32)
    centre = values - jnp.mean(values, axis=0, keepdims=True)
    spread = jnp.mean(centre * centre, axis=0, keepdims=True)
    return centre * lax.rsqrt(spread + EPSILON)


def gelu(x):
    return 0.5 * x * (1.0 + jnp.tanh(0.7978845608028654 * (x + 0.044715 * (x * x * x))))


def greet(partners):
    barrier = pltpu.get_barrier_semaphore()
    for partner in partners:
        pl.semaphore_signal(barrier, inc=1, device_id=partner, device_id_type=MESH)
    pl.semaphore_wait(barrier, len(partners))


def remote(src, dst, sems, index, partner):
    send, recv = sems
    return pltpu.make_async_remote_copy(
        src_ref=src, dst_ref=dst, send_sem=send.at[index], recv_sem=recv.at[index],
        device_id=partner, device_id_type=MESH,
    )


def prologue_kernel(serial_count, level_count, points, marks, slots, q0, k0, v0, o0, m_in, m_out, q1, k1, v1, o1,
                    window, window_marks, slots_all, small, large, send, recv, local):
    s, l, f = lax.axis_index("serial"), lax.axis_index("level"), lax.axis_index("feat")
    other = 1 - f
    shard = s * level_count + l
    total = serial_count * level_count
    beside = lax.rem(shard + 2 * f - 1 + total, total)
    sibling = {"feat": other}
    edge = {"serial": beside // level_count, "level": lax.rem(beside, level_count), "feat": other}
    peers = [{"serial": lax.rem(s + d, serial_count)} for d in range(1, serial_count)]
    greet([sibling, edge] + peers)
    sems = (send, recv)
    rows = points.shape[1]
    kept = rows - PATCH
    src = pl.ds(pl.multiple_of(f * kept, PATCH), PATCH)
    dst = pl.ds(pl.multiple_of(other * kept, PATCH), PATCH)
    copies = [
        remote(points.at[:, src], window.at[:, dst], sems, 0, edge),
        remote(marks.at[:, src], window_marks.at[:, dst], sems, 1, edge),
    ]
    for copy in copies:
        copy.start()
    near = pl.ds(pl.multiple_of(f * PATCH, PATCH), kept)
    here = pl.ds(pl.multiple_of(other * PATCH, PATCH), kept)
    own = [
        pltpu.make_async_copy(points.at[:, near], window.at[:, here], local.at[0]),
        pltpu.make_async_copy(marks.at[:, near], window_marks.at[:, here], local.at[1]),
    ]
    for copy in own:
        copy.start()
    for place, part in enumerate((q0, k0, v0, o0)):
        small[f, place] = part[...]
    for place, part in enumerate((m_in, m_out, q1, k1, v1, o1)):
        large[f, place] = part[...]
    weights = [
        remote(small.at[f], small.at[f], sems, 2, sibling),
        remote(large.at[f], large.at[f], sems, 3, sibling),
    ]
    for copy in weights:
        copy.start()
    slots_all[s] = slots[...]
    for d, peer in enumerate(peers):
        copy = remote(slots, slots_all.at[s], sems, 4 + d, peer)
        copy.start()
        copies.append(copy)
    for copy in own + copies + weights:
        copy.wait()


def swap_kernel(src, out, send, recv):
    f = lax.axis_index("feat")
    sibling = {"feat": 1 - f}
    greet([sibling])
    copy = remote(src, out.at[f], (send, recv), 0, sibling)
    copy.start()
    out[f] = src[...]
    copy.wait()


def fine_kernel(ranges, window, window_marks, small, large, out, keys, values_t, queries_t, scores):
    marks = window_marks[...]
    high = jnp.where((marks < 0) | (marks >= OUTSIDE), HI_ROWS - 1, marks // LO_ROWS)
    low = jnp.where(marks < 0, 0, marks % LO_ROWS)
    total = window.shape[1]
    count = out.shape[1]
    width = window.shape[0]
    heads = width // HEAD
    first = (total - count) // 2
    normed = norm(window[...]).astype(BF16)
    weight = [jnp.concatenate([small[0, i], small[1, i]], axis=0) for i in range(4)]
    queries_t[...] = (dot(weight[0], normed[:, first:first + count]).astype(BF16) * HEAD ** (-0.5)).astype(BF16)
    values_t[...] = dot(weight[2], normed).astype(BF16)
    key_t = dot(weight[1], normed).astype(BF16)
    for start in range(0, total, TILE):
        part = slice(start, start + TILE)
        hot_high = (lax.broadcasted_iota(jnp.int32, (HI_ROWS, TILE), 0) == high[:, part]).astype(F32)
        hot_low = (lax.broadcasted_iota(jnp.int32, (LO_ROWS, TILE), 0) == low[:, part]).astype(F32)
        stacked = jnp.concatenate([key_t[:, part].astype(F32), hot_high, hot_low], axis=0)
        keys[part, :] = jnp.transpose(stacked).astype(BF16)

    def block(index, carry):
        columns = pl.ds(pl.multiple_of(index * TILE, TILE), TILE)
        middle = pl.ds(pl.multiple_of(first + index * TILE, TILE), TILE)
        own = window_marks[:, middle]
        hot_high = lax.broadcasted_iota(jnp.int32, (HI_ROWS, TILE), 0) == own // LO_ROWS
        hot_low = lax.broadcasted_iota(jnp.int32, (LO_ROWS, TILE), 0) == own % LO_ROWS
        barred = jnp.concatenate(
            [jnp.where(hot_high, 0.0, NEG_LARGE), jnp.where(hot_low, 0.0, NEG_LARGE)], axis=0
        ).astype(BF16)
        query = queries_t[:, columns].astype(F32)
        head_of = lax.broadcasted_iota(jnp.int32, (width, TILE), 0) // HEAD
        asked = jnp.concatenate(
            [
                jnp.concatenate([jnp.where(head_of == h, query, 0.0).astype(BF16), barred], axis=0)
                for h in range(heads)
            ],
            axis=1,
        )
        low_tile, high_tile = ranges[2 * index], ranges[2 * index + 1]

        def score(tile, top):
            rows = pl.ds(pl.multiple_of(tile * TILE, TILE), TILE)
            got = dot(keys[rows, :], asked)
            scores[pl.ds(pl.multiple_of((tile - low_tile) * TILE, TILE), TILE), :] = got
            return jnp.maximum(top, jnp.max(got.reshape(TILE // 8, 8, heads * TILE), axis=0))

        top = lax.fori_loop(low_tile, high_tile, score, jnp.full((8, heads * TILE), -3e38, F32))
        top = jnp.max(top, axis=0, keepdims=True)

        def mix(tile, state):
            total_weight, sums = state
            rows = pl.ds(pl.multiple_of((tile - low_tile) * TILE, TILE), TILE)
            places = pl.ds(pl.multiple_of(tile * TILE, TILE), TILE)
            weights = jnp.exp(scores[rows, :] - top)
            total_weight = total_weight + jnp.sum(weights.reshape(TILE // 8, 8, heads * TILE), axis=0)
            rounded = weights.astype(BF16)
            sums = tuple(
                sums[h]
                + dot(values_t[h * HEAD:(h + 1) * HEAD, places], rounded[:, h * TILE:(h + 1) * TILE])
                for h in range(heads)
            )
            return total_weight, sums

        total_weight, sums = lax.fori_loop(
            low_tile, high_tile, mix,
            (jnp.zeros((8, heads * TILE), F32), tuple(jnp.zeros((HEAD, TILE), F32) for _ in range(heads))),
        )
        total_weight = jnp.sum(total_weight, axis=0, keepdims=True)
        mixed = jnp.concatenate(
            [sums[h] / total_weight[:, h * TILE:(h + 1) * TILE] for h in range(heads)], axis=0
        ).astype(BF16)
        hidden = (window[:, middle].astype(F32) + dot(weight[3], mixed, TN)).astype(BF16)
        normed1 = norm(hidden).astype(BF16)
        fed = jnp.zeros((width, TILE), F32)
        for f in range(2):
            inner = gelu(dot(large[f, 0], normed1, TN)).astype(BF16)
            fed = fed + dot(large[f, 1], inner)
        out[:, columns] = (hidden.astype(F32) + fed).astype(BF16)
        return carry

    lax.fori_loop(0, count // TILE, block, 0)


def belongs(starts, ends, offset):
    places = lax.broadcasted_iota(jnp.int32, (TILE, SPAN), 0) + offset
    return jnp.where((places >= starts) & (places < ends), 1.0, 0.0).astype(BF16)


def pool_kernel(lows, fine, starts, ends, out, sums):
    sums[...] = jnp.zeros_like(sums)
    half = fine.shape[2]
    for index in range(2 * half // TILE):
        start = index * TILE
        near = pl.ds(pl.multiple_of(lows[index] * 128, 128), SPAN)
        owner = belongs(starts[:, near], ends[:, near], start)
        block = fine[start // half, :, start % half:start % half + TILE]
        sums[:, near] += dot(block, owner)
    rows = out.shape[1]
    mine = pl.ds(pl.multiple_of(lax.axis_index("feat") * rows, 128), rows)
    members = (ends[:, mine] - starts[:, mine]).astype(F32)
    out[...] = (sums[:, mine] / members).astype(BF16)


def coarse_kernel(serial_count, level_count, part, slots_all, own_slots, large, w_pool, w_up, out,
                  pooled, lifted, landed, keys, queries_t, values_t, nearby, send1, recv1, send2, recv2):
    s, l, f = lax.axis_index("serial"), lax.axis_index("level"), lax.axis_index("feat")
    other = 1 - f
    sibling = {"feat": other}
    peers = [{"serial": lax.rem(s + d, serial_count)} for d in range(1, serial_count)]
    origins = [lax.rem(s + serial_count - d, serial_count) for d in range(serial_count)]
    greet([sibling] + peers)
    count = part.shape[1]
    blocks = count // TILE

    def share(source, slot, send, recv, first):
        sems = (send, recv)
        copies = [remote(source, slot, sems, first, sibling)]
        copies += [remote(source, slot, sems, first + d, peer) for d, peer in enumerate(peers, 1)]
        for copy in copies[1:] + copies[:1]:
            copy.start()
        return copies

    def relay(slot, send, recv, index):
        copy = remote(slot, slot, (send, recv), index, sibling)
        copy.start()
        return copy

    copies = share(part, pooled.at[s, f], send1, recv1, 0)
    pooled[s, f] = part[...]
    base = ((s * level_count + l) * 2 + f) * count
    row = lax.broadcasted_iota(jnp.int32, (TILE, count), 0)
    landed[...] = jnp.zeros_like(landed)

    def land(origin, half):
        values = pooled[origin, half]
        columns = pl.ds(pl.multiple_of(half * count, TILE), count)
        wanted = slots_all[origin, :, columns] - base
        for index in range(blocks):
            chosen = jnp.where(wanted - index * TILE == row, 1.0, 0.0).astype(BF16)
            landed[:, index * TILE:(index + 1) * TILE] += dot(values, chosen, NT)

    land(s, f)
    copies[0].wait_recv()
    land(s, other)
    relays = []
    for d in range(1, serial_count):
        copies[d].wait_recv()
        relays.append(relay(pooled.at[origins[d], f], send1, recv1, serial_count + d - 1))
        land(origins[d], f)
        if d > 1:
            relays[d - 2].wait_recv()
            land(origins[d - 1], other)
    if relays:
        relays[-1].wait_recv()
        land(origins[-1], other)
    for copy in copies + relays:
        copy.wait_send()

    coarse = gelu(norm(dot(w_pool[...], landed[...].astype(BF16), TN))).astype(BF16)
    normed = norm(coarse).astype(BF16)
    weight = [jnp.concatenate([large[0, i], large[1, i]], axis=0) for i in range(2, 6)]
    width = coarse.shape[0]
    heads = width // HEAD
    queries_t[...] = (dot(weight[0], normed).astype(BF16) * HEAD ** (-0.5)).astype(BF16)
    values_t[...] = dot(weight[2], normed).astype(BF16)
    keys[...] = jnp.transpose(dot(weight[1], normed)).astype(BF16)
    head_of = lax.broadcasted_iota(jnp.int32, (width, TILE), 0) // HEAD
    stride = 2 * serial_count - 1
    sent, passed = [], []

    def forward(block):
        got = []
        for d in range(1, serial_count):
            sent[block][d].wait_recv()
            got.append(relay(lifted.at[origins[d], f, block], send2, recv2, block * stride + serial_count + d - 1))
        passed.append(got)

    for block in range(blocks):
        columns = slice(block * TILE, (block + 1) * TILE)
        query = queries_t[:, columns].astype(F32)
        parts = []
        for h in range(heads):
            got = dot(keys[...], jnp.where(head_of == h, query, 0.0).astype(BF16))
            weights = jnp.exp(got - jnp.max(got, axis=0, keepdims=True))
            total = jnp.sum(weights, axis=0, keepdims=True)
            parts.append(dot(values_t[h * HEAD:(h + 1) * HEAD, :], weights.astype(BF16)) / total)
        mixed = jnp.concatenate(parts, axis=0).astype(BF16)
        done = (coarse[:, columns].astype(F32) + dot(weight[3], mixed, TN)).astype(BF16)
        lifted[s, f, block] = dot(w_up[...], done).astype(BF16)
        slot = lifted.at[s, f, block]
        sent.append(share(slot, slot, send2, recv2, block * stride))
        if block > 0:
            forward(block - 1)

    nearby[...] = jnp.zeros_like(nearby)
    square = lax.broadcasted_iota(jnp.int32, (TILE, TILE), 0)

    def arrived(block):
        sent[block][0].wait_recv()
        for copy in passed[block]:
            copy.wait_recv()

    def fetch(chosen_blocks):
        def column(index, carry):
            columns = pl.ds(pl.multiple_of(index * TILE, TILE), TILE)
            wanted = own_slots[:, columns]
            total = nearby[:, columns]
            for origin in range(serial_count):
                for half in range(2):
                    start = ((origin * level_count + l) * 2 + half) * count
                    for block in chosen_blocks:
                        chosen = jnp.where(wanted - (start + block * TILE) == square, 1.0, 0.0).astype(BF16)
                        total = total + dot(lifted[origin, half, block], chosen)
            nearby[:, columns] = total
            return carry

        lax.fori_loop(0, own_slots.shape[1] // TILE, column, 0)

    for block in range(blocks - 2):
        arrived(block)
    fetch(range(blocks - 2))
    forward(blocks - 1)
    arrived(blocks - 2)
    fetch([blocks - 2])
    arrived(blocks - 1)
    fetch([blocks - 1])
    out[...] = nearby[...].astype(BF16)
    for group in sent + passed:
        for copy in group:
            copy.wait_send()


def spread_kernel(lows, nearby, fine, starts, ends, out):
    half = fine.shape[2]
    for index in range(2 * half // TILE):
        start = index * TILE
        near = pl.ds(pl.multiple_of(lows[index] * 128, 128), SPAN)
        owner = belongs(starts[:, near], ends[:, near], start)
        block = fine[start // half, :, start % half:start % half + TILE]
        out[:, start:start + TILE] = (block.astype(F32) + dot(nearby[:, near], owner, NT)).astype(BF16)


def call(kernel, outs, ins, scratch=(), collective=None):
    params = dict(vmem_limit_bytes=VMEM_BYTES)
    if collective is not None:
        params.update(collective_id=collective, has_side_effects=True)
    return pl.pallas_call(
        kernel,
        out_shape=[jax.ShapeDtypeStruct(shape, kind) for shape, kind in outs],
        in_specs=[SMEM if place == "scalar" else VMEM for place, _ in ins],
        out_specs=[VMEM] * len(outs),
        scratch_shapes=list(scratch),
        compiler_params=pltpu.CompilerParams(**params),
    )(*[value for _, value in ins])


def vectors(*values):
    return [("vector", value) for value in values]


def local(points, patch_ids, child_counts, voxel_slot, w_query0, w_key0, w_value0, w_attn_out0, w_mlp_in, w_mlp_out,
          w_pool, w_query1, w_key1, w_value1, w_attn_out1, w_up):
    rows, width = points.shape
    voxels = voxel_slot.shape[0]
    serial_count, level_count = lax.axis_size("serial"), lax.axis_size("level")
    dma = pltpu.SemaphoreType.DMA
    slots = voxel_slot.reshape(1, voxels)
    counts = child_counts.reshape(1, voxels)
    ends = jnp.cumsum(counts, axis=1)
    starts = ends - counts
    tiles = jnp.arange(rows // TILE, dtype=jnp.int32) * TILE
    lows = jnp.minimum(jnp.sum((ends <= tiles[:, None]).astype(jnp.int32), axis=1) // 128, (voxels - SPAN) // 128)

    window, window_marks, slots_all, small, large = call(
        functools.partial(prologue_kernel, serial_count, level_count),
        [
            ((width, rows), BF16), ((1, rows), jnp.int32), ((serial_count, 1, voxels), jnp.int32),
            ((2, 4) + w_query0.shape[::-1], BF16), ((2, 6) + w_mlp_in.shape, BF16),
        ],
        vectors(points.T, patch_ids.reshape(1, rows), slots, w_query0.T, w_key0.T, w_value0.T, w_attn_out0,
                w_mlp_in, w_mlp_out.T, w_query1.T, w_key1.T, w_value1.T, w_attn_out1),
        [dma((3 + serial_count,)), dma((3 + serial_count,)), dma((2,))],
        collective=0,
    )
    shard = lax.axis_index("serial") * level_count + lax.axis_index("level")
    f = lax.axis_index("feat")
    place = jnp.arange(rows, dtype=jnp.int32)[None, :]
    before = (shard == 0) & (f == 0) & (place < PATCH)
    after = (shard == serial_count * level_count - 1) & (f == 1) & (place >= rows - PATCH)
    window_marks = jnp.where(before, -1, jnp.where(after, OUTSIDE, window_marks))
    half = rows // 2
    asked = window_marks[0, half // 2:half // 2 + half].reshape(-1, TILE)
    low = jnp.sum((window_marks < asked[:, :1]).astype(jnp.int32), axis=1) // TILE
    high = (jnp.sum((window_marks <= asked[:, -1:]).astype(jnp.int32), axis=1) + TILE - 1) // TILE
    ranges = jnp.stack([low, high], axis=1).reshape(-1)

    (fine_half,) = call(
        fine_kernel,
        [((width, half), BF16)],
        [("scalar", ranges)] + vectors(window, window_marks, small, large),
        [
            pltpu.VMEM((rows, width + HI_ROWS + LO_ROWS), BF16), pltpu.VMEM((width, rows), BF16),
            pltpu.VMEM((width, half), BF16), pltpu.VMEM((2 * PATCH + TILE, width // HEAD * TILE), F32),
        ],
    )
    (fine,) = call(swap_kernel, [((2, width, half), BF16)], vectors(fine_half), [dma((1,)), dma((1,))], collective=1)
    part = voxels // 2
    (pooled_part,) = call(
        pool_kernel,
        [((width, part), BF16)],
        [("scalar", lows)] + vectors(fine, starts, ends),
        [pltpu.VMEM((width, voxels), F32)],
    )

    wide = w_pool.shape[1]
    blocks = part // TILE
    each = 2 * serial_count - 1
    (nearby,) = call(
        functools.partial(coarse_kernel, serial_count, level_count),
        [((width, voxels), BF16)],
        vectors(pooled_part, slots_all, slots, large, w_pool, w_up.T),
        [
            pltpu.VMEM((serial_count, 2, width, part), BF16), pltpu.VMEM((serial_count, 2, blocks, width, TILE), BF16),
            pltpu.VMEM((width, part), F32), pltpu.VMEM((part, wide), BF16),
            pltpu.VMEM((wide, part), BF16), pltpu.VMEM((wide, part), BF16), pltpu.VMEM((width, voxels), F32),
            dma((each,)), dma((each,)), dma((blocks * each,)), dma((blocks * each,)),
        ],
        collective=2,
    )
    (refined,) = call(
        spread_kernel,
        [((width, rows), BF16)],
        [("scalar", lows)] + vectors(nearby, fine, starts, ends),
    )
    return refined.T


def solution(mesh):
    shards = ("groups", "serial", "level")
    columns, stacked = P(None, "feat"), P("feat", None)
    in_specs = (
        P(shards, None), P(shards), P(shards, None), P(shards),
        columns, columns, columns, stacked, columns, stacked, P(),
        columns, columns, columns, stacked, P(),
    )
    return jax.shard_map(local, mesh=mesh, in_specs=in_specs, out_specs=P(shards, None), check_vma=False)
```

profile of v0, /device:TPU:0, one launch (start us, length us, event | category | flops | bytes accessed | tf_op | source)
XLA Modules:
  0.0 104.1 jit_solution(7227745346258769098)
XLA Ops:
  0.0 0.7 copy-done.15
  0.7 0.3 reduce-window.6
  1.0 0.2 slice_reduce_fusion.1
  1.2 0.2 reduce-window.9
  1.4 0.1 bitcast_add_fusion
  1.4 0.2 convert_reduce_fusion.2
  1.7 0.1 broadcast.186
  1.8 0.3 copy-done.5
  2.1 0.3 copy-done.4
  2.4 0.1 copy-done.1
  2.4 0.0 copy-done.2
  2.5 1.0 copy-done
  3.5 9.4 %shard_map.154 = (bf16[64,4096]{1,0:T(8,128)(2,1)S(1)}, s32[1,4096]{1,0:T(1,128)S(1)}, s32[4,1,2048]{2,1,0:T(1,128)S(1)}, bf16[2,4,32,64]{3,2,1,0:T(8,128)(2,1)S(1)}, bf16[2,6,64,128]{3,2,1,0:T(8,128)(2,1)S(1)}) custom-call(bf16[64,4096]{1,0:T(8,128)(2,1)S(1)} %bitcast.41, s32[1,4096]{1,0:T(1,128)S(1)} %bitcast.45, s32[1,2048]{1,0:T(1,128)S(1)} %bitcast.43, ...), custom_call_target="tpu_custom_call" | custom-call | tf_op jit(solution)/shard_map/pallas_call | solution.py:367
  13.0 0.1 fusion.2
  13.0 0.1 copy.27
  13.1 0.1 copy.26
  13.2 0.2 convert_reduce_fusion.1
  13.5 0.1 copy.25
  13.6 0.1 reshape.194.ranges
  13.6 26.7 %shard_map.155.src = bf16[64,2048]{1,0:T(8,128)(2,1)S(1)} custom-call(s32[16]{0:T(128)S(1)} %reshape.194.ranges, bf16[64,4096]{1,0:T(8,128)(2,1)S(1)} %get-tuple-element.11.window, s32[1,4096]{1,0:T(1,128)S(1)} %and_select_fusion.1.window_marks, bf16[2,4,32,64]{3,2,1,0:T(8,128)(2,1)S(1)} %get-tuple-element.12.small, ...), custom_call_target="tpu_custom_call" | custom-call | tf_op jit(solution)/shard_map/pallas_call | solution.py:367
  40.3 6.8 %shard_map.156.fine = bf16[2,64,2048]{2,1,0:T(8,128)(2,1)S(1)} custom-call(bf16[64,2048]{1,0:T(8,128)(2,1)S(1)} %shard_map.155.src), custom_call_target="tpu_custom_call" | custom-call | tf_op jit(solution)/shard_map/pallas_call | solution.py:367
  47.2 1.7 %shard_map.157.part = bf16[64,1024]{1,0:T(8,128)(2,1)S(1)} custom-call(s32[16]{0:T(128)S(1)} %fusion.lows, bf16[2,64,2048]{2,1,0:T(8,128)(2,1)S(1)} %shard_map.156.fine, s32[1,2048]{1,0:T(1,128)S(1)} %get-tuple-element.17.starts, s32[1,2048]{1,0:T(1,128)S(1)} %get-tuple-element.18.ends), custom_call_target="tpu_custom_call" | custom-call | tf_op jit(solution)/shard_map/pallas_call | solution.py:367
  48.9 52.7 %shard_map.158.nearby = bf16[64,2048]{1,0:T(8,128)(2,1)S(1)} custom-call(bf16[64,1024]{1,0:T(8,128)(2,1)S(1)} %shard_map.157.part, s32[4,1,2048]{2,1,0:T(1,128)S(1)} %get-tuple-element.14.slots_all, s32[1,2048]{1,0:T(1,128)S(1)} %bitcast.44, bf16[2,6,64,128]{3,2,1,0:T(8,128)(2,1)S(1)} %get-tuple-element.13.large, bf16[64,128]{1,0:T(8,128)(2,1)S(1)} %copy-done.9, ...), custom_call_target="tpu_custom_call" | custom-call | tf_op jit(solution)/shard_map/pallas_call | solution.py:367
  101.6 2.5 %shard_map.159 = bf16[64,4096]{1,0:T(8,128)(2,1)} custom-call(s32[16]{0:T(128)S(1)} %fusion.lows, bf16[64,2048]{1,0:T(8,128)(2,1)S(1)} %shard_map.158.nearby, bf16[2,64,2048]{2,1,0:T(8,128)(2,1)S(1)} %shard_map.156.fine, s32[1,2048]{1,0:T(1,128)S(1)} %get-tuple-element.17.starts, s32[1,2048]{1,0:T(1,128)S(1)} %get-tuple-element.18.ends), custom_call_target="tpu_custom_call" | custom-call | tf_op jit(solution)/shard_map/pallas_call | solution.py:367
  (35 shorter events, 0.2 us)
Async XLA Ops:
  0.0 0.7 copy-start.15
  0.0 1.8 %copy-start.14 = (bf16[32,64]{1,0:T(8,128)(2,1)S(1)}, bf16[32,64]{1,0:T(8,128)(2,1)}, u32[]{:S(2)}) copy-start(bf16[32,64]{1,0:T(8,128)(2,1)} %o0.1) | copy-start | bytes 12292
  0.0 1.8 %copy-start.13 = (bf16[64,32]{0,1:T(8,128)(2,1)S(1)}, bf16[64,32]{0,1:T(8,128)(2,1)}, u32[]{:S(2)}) copy-start(bf16[64,32]{0,1:T(8,128)(2,1)} %param.22) | copy-start | bytes 12292
  0.0 1.8 %copy-start.12 = (bf16[64,32]{0,1:T(8,128)(2,1)S(1)}, bf16[64,32]{0,1:T(8,128)(2,1)}, u32[]{:S(2)}) copy-start(bf16[64,32]{0,1:T(8,128)(2,1)} %param.21) | copy-start | bytes 12292
  0.0 1.8 %copy-start.11 = (bf16[64,32]{0,1:T(8,128)(2,1)S(1)}, bf16[64,32]{0,1:T(8,128)(2,1)}, u32[]{:S(2)}) copy-start(bf16[64,32]{0,1:T(8,128)(2,1)} %param.20) | copy-start | bytes 12292
  0.0 1.8 %copy-start.8 = (bf16[64,128]{1,0:T(8,128)(2,1)S(1)}, bf16[64,128]{1,0:T(8,128)(2,1)}, u32[]{:S(2)}) copy-start(bf16[64,128]{1,0:T(8,128)(2,1)} %o1.1) | copy-start | bytes 49156
  0.7 1.1 %copy-start.7 = (bf16[128,64]{0,1:T(8,128)(2,1)S(1)}, bf16[128,64]{0,1:T(8,128)(2,1)}, u32[]{:S(2)}) copy-start(bf16[128,64]{0,1:T(8,128)(2,1)} %param.29) | copy-start | bytes 49156
  1.0 0.8 copy-start.6
  1.4 0.7 copy-start.5
  1.6 0.7 copy-start.4
  1.7 0.7 copy-start.1
  1.7 0.7 copy-start.2
  1.7 0.8 copy-start.3
  2.5 1.0 %copy-start = (bf16[4096,64]{0,1:T(8,128)(2,1)S(1)}, bf16[4096,64]{0,1:T(8,128)(2,1)}, u32[]{:S(2)}) copy-start(bf16[4096,64]{0,1:T(8,128)(2,1)} %param.16) | copy-start | bytes 1572868
  47.2 1.7 %copy-start.9 = (bf16[64,128]{1,0:T(8,128)(2,1)S(1)}, bf16[64,128]{1,0:T(8,128)(2,1)}, u32[]{:S(2)}) copy-start(bf16[64,128]{1,0:T(8,128)(2,1)} %w_pool.1) | copy-start | bytes 49156
  47.2 1.7 %copy-start.10 = (bf16[128,64]{0,1:T(8,128)(2,1)S(1)}, bf16[128,64]{0,1:T(8,128)(2,1)}, u32[]{:S(2)}) copy-start(bf16[128,64]{0,1:T(8,128)(2,1)} %param.31) | copy-start | bytes 49156
where the time goes:
time: 103 us; the launch traced here: 104 us
  Pallas kernels  99.8 us (97%)
  local copies, waits for them, and re-layouts  3.09 us (3%)
  other arithmetic  1.06 us (1%)
    pallas_call x6, Pallas kernels, call(): pl.pallas_call(kernel, out_shape=[jax.ShapeDtypeStruct(shape, kind) for s...  99.8 us
    unnamed x34, local copies, waits for them, and re-layouts  2.57 us

commit v1 on v0

--- a/solution.py
+++ b/solution.py
@@ -14,7 +14,10 @@
 TILE = 256
 SPAN = 384
 HI_ROWS = 64
-LO_ROWS = 128
+LO_ROWS = 64
+BOUND = 64.0
+UNIT = 1.4426950408889634 * HEAD ** (-0.5)
+VALUE_ROWS = 2 * HEAD
 OUTSIDE = 1 << 20
 MESH = pl.DeviceIdType.MESH
 BF16 = jnp.bfloat16
@@ -41,6 +44,18 @@
 
 def gelu(x):
     return 0.5 * x * (1.0 + jnp.tanh(0.7978845608028654 * (x + 0.044715 * (x * x * x))))
+
+
+def in_parts(query, kept, factor):
+    scaled = jnp.where(kept, query.astype(F32) * factor, 0.0)
+    high = scaled.astype(BF16)
+    return [high, (scaled - high.astype(F32)).astype(BF16)]
+
+
+def with_ones(values, head):
+    own = values[head * HEAD:(head + 1) * HEAD, :]
+    extra = (lax.broadcasted_iota(jnp.int32, own.shape, 0) == 0).astype(BF16)
+    return [own, extra]
 
 
 def greet(partners):
@@ -128,15 +143,25 @@
     first = (total - count) // 2
     normed = norm(window[...]).astype(BF16)
     weight = [jnp.concatenate([small[0, i], small[1, i]], axis=0) for i in range(4)]
-    queries_t[...] = (dot(weight[0], normed[:, first:first + count]).astype(BF16) * HEAD ** (-0.5)).astype(BF16)
-    values_t[...] = dot(weight[2], normed).astype(BF16)
+    queries_t[...] = dot(weight[0], normed[:, first:first + count]).astype(BF16)
+    value_t = dot(weight[2], normed).astype(BF16)
+    values_t[...] = jnp.concatenate([rows for h in range(heads) for rows in with_ones(value_t, h)], axis=0)
     key_t = dot(weight[1], normed).astype(BF16)
+
+    def longest(rows):
+        squares = jnp.square(rows.astype(F32))
+        return jnp.max(jnp.sum(squares.reshape(heads, HEAD, rows.shape[1]), axis=1))
+
+    small_scores = longest(queries_t[...]) * longest(key_t) * UNIT ** 2 <= BOUND ** 2
     for start in range(0, total, TILE):
         part = slice(start, start + TILE)
         hot_high = (lax.broadcasted_iota(jnp.int32, (HI_ROWS, TILE), 0) == high[:, part]).astype(F32)
         hot_low = (lax.broadcasted_iota(jnp.int32, (LO_ROWS, TILE), 0) == low[:, part]).astype(F32)
-        stacked = jnp.concatenate([key_t[:, part].astype(F32), hot_high, hot_low], axis=0)
+        key = key_t[:, part].astype(F32)
+        stacked = jnp.concatenate([key, key, hot_high, hot_low], axis=0)
         keys[part, :] = jnp.transpose(stacked).astype(BF16)
+
+    factor = jnp.where(small_scores, UNIT, HEAD ** (-0.5))
 
     def block(index, carry):
         columns = pl.ds(pl.multiple_of(index * TILE, TILE), TILE)
@@ -147,48 +172,52 @@
         barred = jnp.concatenate(
             [jnp.where(hot_high, 0.0, NEG_LARGE), jnp.where(hot_low, 0.0, NEG_LARGE)], axis=0
         ).astype(BF16)
-        query = queries_t[:, columns].astype(F32)
+        query = queries_t[:, columns]
         head_of = lax.broadcasted_iota(jnp.int32, (width, TILE), 0) // HEAD
         asked = jnp.concatenate(
-            [
-                jnp.concatenate([jnp.where(head_of == h, query, 0.0).astype(BF16), barred], axis=0)
-                for h in range(heads)
-            ],
-            axis=1,
+            [jnp.concatenate(in_parts(query, head_of == h, factor) + [barred], axis=0) for h in range(heads)], axis=1
         )
         low_tile, high_tile = ranges[2 * index], ranges[2 * index + 1]
 
-        def score(tile, top):
-            rows = pl.ds(pl.multiple_of(tile * TILE, TILE), TILE)
-            got = dot(keys[rows, :], asked)
-            scores[pl.ds(pl.multiple_of((tile - low_tile) * TILE, TILE), TILE), :] = got
-            return jnp.maximum(top, jnp.max(got.reshape(TILE // 8, 8, heads * TILE), axis=0))
-
-        top = lax.fori_loop(low_tile, high_tile, score, jnp.full((8, heads * TILE), -3e38, F32))
-        top = jnp.max(top, axis=0, keepdims=True)
-
-        def mix(tile, state):
-            total_weight, sums = state
-            rows = pl.ds(pl.multiple_of((tile - low_tile) * TILE, TILE), TILE)
+        def blend(tile, weights, sums):
             places = pl.ds(pl.multiple_of(tile * TILE, TILE), TILE)
-            weights = jnp.exp(scores[rows, :] - top)
-            total_weight = total_weight + jnp.sum(weights.reshape(TILE // 8, 8, heads * TILE), axis=0)
-            rounded = weights.astype(BF16)
-            sums = tuple(
+            return tuple(
                 sums[h]
-                + dot(values_t[h * HEAD:(h + 1) * HEAD, places], rounded[:, h * TILE:(h + 1) * TILE])
+                + dot(
+                    values_t[h * VALUE_ROWS:(h + 1) * VALUE_ROWS, places],
+                    weights[:, h * TILE:(h + 1) * TILE],
+                )
                 for h in range(heads)
             )
-            return total_weight, sums
-
-        total_weight, sums = lax.fori_loop(
-            low_tile, high_tile, mix,
-            (jnp.zeros((8, heads * TILE), F32), tuple(jnp.zeros((HEAD, TILE), F32) for _ in range(heads))),
-        )
-        total_weight = jnp.sum(total_weight, axis=0, keepdims=True)
-        mixed = jnp.concatenate(
-            [sums[h] / total_weight[:, h * TILE:(h + 1) * TILE] for h in range(heads)], axis=0
-        ).astype(BF16)
+
+        def score(tile):
+            return dot(keys[pl.ds(pl.multiple_of(tile * TILE, TILE), TILE), :], asked)
+
+        nothing = tuple(jnp.zeros((VALUE_ROWS, TILE), F32) for _ in range(heads))
+
+        def unshifted():
+            def step(tile, sums):
+                return blend(tile, jnp.exp2(score(tile)).astype(BF16), sums)
+
+            return lax.fori_loop(low_tile, high_tile, step, nothing)
+
+        def shifted():
+            def rank(tile, top):
+                got = score(tile)
+                scores[pl.ds(pl.multiple_of((tile - low_tile) * TILE, TILE), TILE), :] = got
+                return jnp.maximum(top, jnp.max(got.reshape(TILE // 8, 8, heads * TILE), axis=0))
+
+            top = lax.fori_loop(low_tile, high_tile, rank, jnp.full((8, heads * TILE), -3e38, F32))
+            top = jnp.max(top, axis=0, keepdims=True)
+
+            def step(tile, sums):
+                rows = pl.ds(pl.multiple_of((tile - low_tile) * TILE, TILE), TILE)
+                return blend(tile, jnp.exp(scores[rows, :] - top).astype(BF16), sums)
+
+            return lax.fori_loop(low_tile, high_tile, step, nothing)
+
+        sums = lax.cond(small_scores, unshifted, shifted)
+        mixed = jnp.concatenate([part[:HEAD] / part[HEAD:HEAD + 1] for part in sums], axis=0).astype(BF16)
         hidden = (window[:, middle].astype(F32) + dot(weight[3], mixed, TN)).astype(BF16)
         normed1 = norm(hidden).astype(BF16)
         fed = jnp.zeros((width, TILE), F32)
@@ -282,7 +311,8 @@
     width = coarse.shape[0]
     heads = width // HEAD
     queries_t[...] = (dot(weight[0], normed).astype(BF16) * HEAD ** (-0.5)).astype(BF16)
-    values_t[...] = dot(weight[2], normed).astype(BF16)
+    value_t = dot(weight[2], normed).astype(BF16)
+    values_t[...] = jnp.concatenate([rows for h in range(heads) for rows in with_ones(value_t, h)], axis=0)
     keys[...] = jnp.transpose(dot(weight[1], normed)).astype(BF16)
     head_of = lax.broadcasted_iota(jnp.int32, (width, TILE), 0) // HEAD
     stride = 2 * serial_count - 1
@@ -301,9 +331,9 @@
         parts = []
         for h in range(heads):
             got = dot(keys[...], jnp.where(head_of == h, query, 0.0).astype(BF16))
-            weights = jnp.exp(got - jnp.max(got, axis=0, keepdims=True))
-            total = jnp.sum(weights, axis=0, keepdims=True)
-            parts.append(dot(values_t[h * HEAD:(h + 1) * HEAD, :], weights.astype(BF16)) / total)
+            weights = jnp.exp(got - jnp.max(got, axis=0, keepdims=True)).astype(BF16)
+            sums = dot(values_t[h * VALUE_ROWS:(h + 1) * VALUE_ROWS, :], weights)
+            parts.append(sums[:HEAD] / sums[HEAD:HEAD + 1])
         mixed = jnp.concatenate(parts, axis=0).astype(BF16)
         done = (coarse[:, columns].astype(F32) + dot(weight[3], mixed, TN)).astype(BF16)
         lifted[s, f, block] = dot(w_up[...], done).astype(BF16)
@@ -419,7 +449,7 @@
         [((width, half), BF16)],
         [("scalar", ranges)] + vectors(window, window_marks, small, large),
         [
-            pltpu.VMEM((rows, width + HI_ROWS + LO_ROWS), BF16), pltpu.VMEM((width, rows), BF16),
+            pltpu.VMEM((rows, 2 * width + HI_ROWS + LO_ROWS), BF16), pltpu.VMEM((2 * width, rows), BF16),
             pltpu.VMEM((width, half), BF16), pltpu.VMEM((2 * PATCH + TILE, width // HEAD * TILE), F32),
         ],
     )
@@ -442,7 +472,7 @@
         [
             pltpu.VMEM((serial_count, 2, width, part), BF16), pltpu.VMEM((serial_count, 2, blocks, width, TILE), BF16),
             pltpu.VMEM((width, part), F32), pltpu.VMEM((part, wide), BF16),
-            pltpu.VMEM((wide, part), BF16), pltpu.VMEM((wide, part), BF16), pltpu.VMEM((width, voxels), F32),
+            pltpu.VMEM((wide, part), BF16), pltpu.VMEM((2 * wide, part), BF16), pltpu.VMEM((width, voxels), F32),
             dma((each,)), dma((each,)), dma((blocks * each,)), dma((blocks * each,)),
         ],
         collective=2,

time: 103 us -> 105 us (1.019); the launches traced: 104 us -> 104 us
  no operation moved by 1% of the time
where the time goes in v1:
time: 105 us; the launch traced here: 104 us
  Pallas kernels  99.4 us (95%)
  local copies, waits for them, and re-layouts  3.09 us (3%)
  other arithmetic  1.06 us (1%)
    pallas_call x6, Pallas kernels, call(): pl.pallas_call(kernel, out_shape=[jax.ShapeDtypeStruct(shape, kind) for s...  99.4 us
    unnamed x34, local copies, waits for them, and re-layouts  2.57 us

profile of v1, /device:TPU:0, one launch (start us, length us, event | category | flops | bytes accessed | tf_op | source)
XLA Modules:
  0.0 103.7 jit_solution(6890688954268835134)
XLA Ops:
  0.0 0.7 copy-done.15
  0.7 0.3 reduce-window.6
  1.0 0.2 slice_reduce_fusion.1
  1.2 0.2 reduce-window.9
  1.4 0.1 bitcast_add_fusion
  1.4 0.2 convert_reduce_fusion.2
  1.7 0.1 broadcast.186
  1.8 0.3 copy-done.5
  2.1 0.3 copy-done.4
  2.4 0.1 copy-done.1
  2.4 0.0 copy-done.2
  2.5 1.0 %copy-done = bf16[4096,64]{0,1:T(8,128)(2,1)S(1)} copy-done((bf16[4096,64]{0,1:T(8,128)(2,1)S(1)}, bf16[4096,64]{0,1:T(8,128)(2,1)}, u32[]{:S(2)}) %copy-start) | copy-done | bytes 524312
  3.5 9.4 %shard_map.154 = (bf16[64,4096]{1,0:T(8,128)(2,1)S(1)}, s32[1,4096]{1,0:T(1,128)S(1)}, s32[4,1,2048]{2,1,0:T(1,128)S(1)}, bf16[2,4,32,64]{3,2,1,0:T(8,128)(2,1)S(1)}, bf16[2,6,64,128]{3,2,1,0:T(8,128)(2,1)S(1)}) custom-call(bf16[64,4096]{1,0:T(8,128)(2,1)S(1)} %bitcast.41, s32[1,4096]{1,0:T(1,128)S(1)} %bitcast.45, s32[1,2048]{1,0:T(1,128)S(1)} %bitcast.43, ...), custom_call_target="tpu_custom_call" | custom-call | tf_op jit(solution)/shard_map/pallas_call | solution.py:397
  13.0 0.1 fusion.2
  13.0 0.1 copy.27
  13.1 0.1 copy.26
  13.2 0.2 convert_reduce_fusion.1
  13.5 0.1 copy.25
  13.6 0.1 reshape.194.ranges
  13.6 29.2 %shard_map.155.src = bf16[64,2048]{1,0:T(8,128)(2,1)S(1)} custom-call(s32[16]{0:T(128)S(1)} %reshape.194.ranges, bf16[64,4096]{1,0:T(8,128)(2,1)S(1)} %get-tuple-element.11.window, s32[1,4096]{1,0:T(1,128)S(1)} %and_select_fusion.1.window_marks, bf16[2,4,32,64]{3,2,1,0:T(8,128)(2,1)S(1)} %get-tuple-element.12.small, ...), custom_call_target="tpu_custom_call" | custom-call | tf_op jit(solution)/shard_map/pallas_call | solution.py:397
  42.9 1.6 %shard_map.156.fine = bf16[2,64,2048]{2,1,0:T(8,128)(2,1)S(1)} custom-call(bf16[64,2048]{1,0:T(8,128)(2,1)S(1)} %shard_map.155.src), custom_call_target="tpu_custom_call" | custom-call | tf_op jit(solution)/shard_map/pallas_call | solution.py:397
  44.5 1.7 %shard_map.157.part = bf16[64,1024]{1,0:T(8,128)(2,1)S(1)} custom-call(s32[16]{0:T(128)S(1)} %fusion.lows, bf16[2,64,2048]{2,1,0:T(8,128)(2,1)S(1)} %shard_map.156.fine, s32[1,2048]{1,0:T(1,128)S(1)} %get-tuple-element.17.starts, s32[1,2048]{1,0:T(1,128)S(1)} %get-tuple-element.18.ends), custom_call_target="tpu_custom_call" | custom-call | tf_op jit(solution)/shard_map/pallas_call | solution.py:397
  46.2 55.0 %shard_map.158.nearby = bf16[64,2048]{1,0:T(8,128)(2,1)S(1)} custom-call(bf16[64,1024]{1,0:T(8,128)(2,1)S(1)} %shard_map.157.part, s32[4,1,2048]{2,1,0:T(1,128)S(1)} %get-tuple-element.14.slots_all, s32[1,2048]{1,0:T(1,128)S(1)} %bitcast.44, bf16[2,6,64,128]{3,2,1,0:T(8,128)(2,1)S(1)} %get-tuple-element.13.large, bf16[64,128]{1,0:T(8,128)(2,1)S(1)} %copy-done.9, ...), custom_call_target="tpu_custom_call" | custom-call | tf_op jit(solution)/shard_map/pallas_call | solution.py:397
  101.2 2.5 %shard_map.159 = bf16[64,4096]{1,0:T(8,128)(2,1)} custom-call(s32[16]{0:T(128)S(1)} %fusion.lows, bf16[64,2048]{1,0:T(8,128)(2,1)S(1)} %shard_map.158.nearby, bf16[2,64,2048]{2,1,0:T(8,128)(2,1)S(1)} %shard_map.156.fine, s32[1,2048]{1,0:T(1,128)S(1)} %get-tuple-element.17.starts, s32[1,2048]{1,0:T(1,128)S(1)} %get-tuple-element.18.ends), custom_call_target="tpu_custom_call" | custom-call | tf_op jit(solution)/shard_map/pallas_call | solution.py:397
  (35 shorter events, 0.2 us)
Async XLA Ops:
  0.0 0.7 copy-start.15
  0.0 1.8 %copy-start.14 = (bf16[32,64]{1,0:T(8,128)(2,1)S(1)}, bf16[32,64]{1,0:T(8,128)(2,1)}, u32[]{:S(2)}) copy-start(bf16[32,64]{1,0:T(8,128)(2,1)} %o0.1) | copy-start | bytes 12292
  0.0 1.8 %copy-start.13 = (bf16[64,32]{0,1:T(8,128)(2,1)S(1)}, bf16[64,32]{0,1:T(8,128)(2,1)}, u32[]{:S(2)}) copy-start(bf16[64,32]{0,1:T(8,128)(2,1)} %param.22) | copy-start | bytes 12292
  0.0 1.8 %copy-start.12 = (bf16[64,32]{0,1:T(8,128)(2,1)S(1)}, bf16[64,32]{0,1:T(8,128)(2,1)}, u32[]{:S(2)}) copy-start(bf16[64,32]{0,1:T(8,128)(2,1)} %param.21) | copy-start | bytes 12292
  0.0 1.8 %copy-start.11 = (bf16[64,32]{0,1:T(8,128)(2,1)S(1)}, bf16[64,32]{0,1:T(8,128)(2,1)}, u32[]{:S(2)}) copy-start(bf16[64,32]{0,1:T(8,128)(2,1)} %param.20) | copy-start | bytes 12292
  0.0 1.8 %copy-start.8 = (bf16[64,128]{1,0:T(8,128)(2,1)S(1)}, bf16[64,128]{1,0:T(8,128)(2,1)}, u32[]{:S(2)}) copy-start(bf16[64,128]{1,0:T(8,128)(2,1)} %o1.1) | copy-start | bytes 49156
  0.7 1.1 %copy-start.7 = (bf16[128,64]{0,1:T(8,128)(2,1)S(1)}, bf16[128,64]{0,1:T(8,128)(2,1)}, u32[]{:S(2)}) copy-start(bf16[128,64]{0,1:T(8,128)(2,1)} %param.29) | copy-start | bytes 49156
  1.0 0.8 copy-start.6
  1.4 0.7 copy-start.5
  1.6 0.7 copy-start.4
  1.7 0.7 copy-start.1
  1.7 0.7 copy-start.2
  1.7 0.8 copy-start.3
  2.5 1.0 %copy-start = (bf16[4096,64]{0,1:T(8,128)(2,1)S(1)}, bf16[4096,64]{0,1:T(8,128)(2,1)}, u32[]{:S(2)}) copy-start(bf16[4096,64]{0,1:T(8,128)(2,1)} %param.16) | copy-start | bytes 1572868
  44.5 1.7 %copy-start.9 = (bf16[64,128]{1,0:T(8,128)(2,1)S(1)}, bf16[64,128]{1,0:T(8,128)(2,1)}, u32[]{:S(2)}) copy-start(bf16[64,128]{1,0:T(8,128)(2,1)} %w_pool.1) | copy-start | bytes 49156
  44.5 1.7 %copy-start.10 = (bf16[128,64]{0,1:T(8,128)(2,1)S(1)}, bf16[128,64]{0,1:T(8,128)(2,1)}, u32[]{:S(2)}) copy-start(bf16[128,64]{0,1:T(8,128)(2,1)} %param.31) | copy-start | bytes 49156

commit v2 on v0

--- a/solution.py
+++ b/solution.py
@@ -13,6 +13,7 @@
 NEG_LARGE = -1e30
 TILE = 256
 SPAN = 384
+STACK = 2
 HI_ROWS = 64
 LO_ROWS = 128
 OUTSIDE = 1 << 20
@@ -222,7 +223,7 @@
 
 
 def coarse_kernel(serial_count, level_count, part, slots_all, own_slots, large, w_pool, w_up, out,
-                  pooled, lifted, landed, keys, queries_t, values_t, nearby, send1, recv1, send2, recv2):
+                  pooled, lifted, landed, keys_t, queries, values, nearby, send1, recv1, send2, recv2):
     s, l, f = lax.axis_index("serial"), lax.axis_index("level"), lax.axis_index("feat")
     other = 1 - f
     sibling = {"feat": other}
@@ -281,10 +282,11 @@
     weight = [jnp.concatenate([large[0, i], large[1, i]], axis=0) for i in range(2, 6)]
     width = coarse.shape[0]
     heads = width // HEAD
-    queries_t[...] = (dot(weight[0], normed).astype(BF16) * HEAD ** (-0.5)).astype(BF16)
-    values_t[...] = dot(weight[2], normed).astype(BF16)
-    keys[...] = jnp.transpose(dot(weight[1], normed)).astype(BF16)
-    head_of = lax.broadcasted_iota(jnp.int32, (width, TILE), 0) // HEAD
+    normed_rows = jnp.transpose(normed.astype(F32)).astype(BF16)
+    queries[...] = (dot(normed_rows, weight[0], NT).astype(BF16) * HEAD ** (-0.5)).astype(BF16)
+    values[...] = dot(normed_rows, weight[2], NT).astype(BF16)
+    keys_t[...] = dot(weight[1], normed).astype(BF16)
+    head_of = lax.broadcasted_iota(jnp.int32, (TILE, width), 1) // HEAD
     stride = 2 * serial_count - 1
     sent, passed = [], []
 
@@ -297,14 +299,18 @@
 
     for block in range(blocks):
         columns = slice(block * TILE, (block + 1) * TILE)
-        query = queries_t[:, columns].astype(F32)
-        parts = []
-        for h in range(heads):
-            got = dot(keys[...], jnp.where(head_of == h, query, 0.0).astype(BF16))
-            weights = jnp.exp(got - jnp.max(got, axis=0, keepdims=True))
-            total = jnp.sum(weights, axis=0, keepdims=True)
-            parts.append(dot(values_t[h * HEAD:(h + 1) * HEAD, :], weights.astype(BF16)) / total)
-        mixed = jnp.concatenate(parts, axis=0).astype(BF16)
+        query = queries[columns, :].astype(F32)
+        mixed = jnp.zeros((TILE, width), F32)
+        for first in range(0, heads, STACK):
+            asked = jnp.concatenate(
+                [jnp.where(head_of == first + i, query, 0.0).astype(BF16) for i in range(STACK)], axis=0
+            )
+            got = dot(asked, keys_t[...])
+            weights = jnp.exp(got - jnp.max(got, axis=1, keepdims=True))
+            sums = dot(weights.astype(BF16), values[...]) / jnp.sum(weights, axis=1, keepdims=True)
+            for i in range(STACK):
+                mixed = jnp.where(head_of == first + i, sums[i * TILE:(i + 1) * TILE], mixed)
+        mixed = jnp.transpose(mixed).astype(BF16)
         done = (coarse[:, columns].astype(F32) + dot(weight[3], mixed, TN)).astype(BF16)
         lifted[s, f, block] = dot(w_up[...], done).astype(BF16)
         slot = lifted.at[s, f, block]
@@ -441,8 +447,8 @@
         vectors(pooled_part, slots_all, slots, large, w_pool, w_up.T),
         [
             pltpu.VMEM((serial_count, 2, width, part), BF16), pltpu.VMEM((serial_count, 2, blocks, width, TILE), BF16),
-            pltpu.VMEM((width, part), F32), pltpu.VMEM((part, wide), BF16),
-            pltpu.VMEM((wide, part), BF16), pltpu.VMEM((wide, part), BF16), pltpu.VMEM((width, voxels), F32),
+            pltpu.VMEM((width, part), F32), pltpu.VMEM((wide, part), BF16),
+            pltpu.VMEM((part, wide), BF16), pltpu.VMEM((part, wide), BF16), pltpu.VMEM((width, voxels), F32),
             dma((each,)), dma((each,)), dma((blocks * each,)), dma((blocks * each,)),
         ],
         collective=2,

time: 103 us -> 97.6 us (0.948)
  Pallas kernels: 99.8 us -> 93.5 us
    pallas_call x6, Pallas kernels: 99.8 us -> 93.5 us  [call(): pl.pallas_call(kernel, out_shape=[jax.ShapeDtypeStruct(shape, kind) for s...]
where the time goes in v2:
time: 97.6 us; the launch traced here: 97.9 us
  Pallas kernels  93.5 us (96%)
  local copies, waits for them, and re-layouts  3.09 us (3%)
  other arithmetic  1.06 us (1%)
    pallas_call x6, Pallas kernels, call(): pl.pallas_call(kernel, out_shape=[jax.ShapeDtypeStruct(shape, kind) for s...  93.5 us
    unnamed x34, local copies, waits for them, and re-layouts  2.57 us

profile of v2, /device:TPU:0, one launch (start us, length us, event | category | flops | bytes accessed | tf_op | source)
XLA Modules:
  0.0 97.9 jit_solution(8116756760969886579)
XLA Ops:
  0.0 0.7 copy-done.15
  0.7 0.3 reduce-window.6
  1.0 0.2 slice_reduce_fusion.1
  1.2 0.2 reduce-window.9
  1.4 0.1 bitcast_add_fusion
  1.4 0.2 convert_reduce_fusion.2
  1.7 0.1 broadcast.186
  1.8 0.3 copy-done.5
  2.1 0.3 copy-done.4
  2.4 0.1 copy-done.1
  2.4 0.0 copy-done.2
  2.5 1.0 %copy-done = bf16[4096,64]{0,1:T(8,128)(2,1)S(1)} copy-done((bf16[4096,64]{0,1:T(8,128)(2,1)S(1)}, bf16[4096,64]{0,1:T(8,128)(2,1)}, u32[]{:S(2)}) %copy-start) | copy-done | bytes 524312
  3.5 9.4 %shard_map.154 = (bf16[64,4096]{1,0:T(8,128)(2,1)S(1)}, s32[1,4096]{1,0:T(1,128)S(1)}, s32[4,1,2048]{2,1,0:T(1,128)S(1)}, bf16[2,4,32,64]{3,2,1,0:T(8,128)(2,1)S(1)}, bf16[2,6,64,128]{3,2,1,0:T(8,128)(2,1)S(1)}) custom-call(bf16[64,4096]{1,0:T(8,128)(2,1)S(1)} %bitcast.41, s32[1,4096]{1,0:T(1,128)S(1)} %bitcast.45, s32[1,2048]{1,0:T(1,128)S(1)} %bitcast.43, ...), custom_call_target="tpu_custom_call" | custom-call | tf_op jit(solution)/shard_map/pallas_call | solution.py:373
  13.0 0.1 fusion.2
  13.0 0.1 copy.27
  13.1 0.1 copy.26
  13.2 0.2 convert_reduce_fusion.1
  13.5 0.1 copy.25
  13.6 0.1 reshape.194.ranges
  13.6 27.8 %shard_map.155.src = bf16[64,2048]{1,0:T(8,128)(2,1)S(1)} custom-call(s32[16]{0:T(128)S(1)} %reshape.194.ranges, bf16[64,4096]{1,0:T(8,128)(2,1)S(1)} %get-tuple-element.11.window, s32[1,4096]{1,0:T(1,128)S(1)} %and_select_fusion.1.window_marks, bf16[2,4,32,64]{3,2,1,0:T(8,128)(2,1)S(1)} %get-tuple-element.12.small, ...), custom_call_target="tpu_custom_call" | custom-call | tf_op jit(solution)/shard_map/pallas_call | solution.py:373
  41.5 2.7 %shard_map.156.fine = bf16[2,64,2048]{2,1,0:T(8,128)(2,1)S(1)} custom-call(bf16[64,2048]{1,0:T(8,128)(2,1)S(1)} %shard_map.155.src), custom_call_target="tpu_custom_call" | custom-call | tf_op jit(solution)/shard_map/pallas_call | solution.py:373
  44.2 1.7 %shard_map.157.part = bf16[64,1024]{1,0:T(8,128)(2,1)S(1)} custom-call(s32[16]{0:T(128)S(1)} %fusion.lows, bf16[2,64,2048]{2,1,0:T(8,128)(2,1)S(1)} %shard_map.156.fine, s32[1,2048]{1,0:T(1,128)S(1)} %get-tuple-element.17.starts, s32[1,2048]{1,0:T(1,128)S(1)} %get-tuple-element.18.ends), custom_call_target="tpu_custom_call" | custom-call | tf_op jit(solution)/shard_map/pallas_call | solution.py:373
  45.9 49.4 %shard_map.158.nearby = bf16[64,2048]{1,0:T(8,128)(2,1)S(1)} custom-call(bf16[64,1024]{1,0:T(8,128)(2,1)S(1)} %shard_map.157.part, s32[4,1,2048]{2,1,0:T(1,128)S(1)} %get-tuple-element.14.slots_all, s32[1,2048]{1,0:T(1,128)S(1)} %bitcast.44, bf16[2,6,64,128]{3,2,1,0:T(8,128)(2,1)S(1)} %get-tuple-element.13.large, bf16[64,128]{1,0:T(8,128)(2,1)S(1)} %copy-done.9, ...), custom_call_target="tpu_custom_call" | custom-call | tf_op jit(solution)/shard_map/pallas_call | solution.py:373
  95.4 2.5 %shard_map.159 = bf16[64,4096]{1,0:T(8,128)(2,1)} custom-call(s32[16]{0:T(128)S(1)} %fusion.lows, bf16[64,2048]{1,0:T(8,128)(2,1)S(1)} %shard_map.158.nearby, bf16[2,64,2048]{2,1,0:T(8,128)(2,1)S(1)} %shard_map.156.fine, s32[1,2048]{1,0:T(1,128)S(1)} %get-tuple-element.17.starts, s32[1,2048]{1,0:T(1,128)S(1)} %get-tuple-element.18.ends), custom_call_target="tpu_custom_call" | custom-call | tf_op jit(solution)/shard_map/pallas_call | solution.py:373
  (35 shorter events, 0.2 us)
Async XLA Ops:
  0.0 0.7 copy-start.15
  0.0 1.8 %copy-start.14 = (bf16[32,64]{1,0:T(8,128)(2,1)S(1)}, bf16[32,64]{1,0:T(8,128)(2,1)}, u32[]{:S(2)}) copy-start(bf16[32,64]{1,0:T(8,128)(2,1)} %o0.1) | copy-start | bytes 12292
  0.0 1.8 %copy-start.13 = (bf16[64,32]{0,1:T(8,128)(2,1)S(1)}, bf16[64,32]{0,1:T(8,128)(2,1)}, u32[]{:S(2)}) copy-start(bf16[64,32]{0,1:T(8,128)(2,1)} %param.22) | copy-start | bytes 12292
  0.0 1.8 %copy-start.12 = (bf16[64,32]{0,1:T(8,128)(2,1)S(1)}, bf16[64,32]{0,1:T(8,128)(2,1)}, u32[]{:S(2)}) copy-start(bf16[64,32]{0,1:T(8,128)(2,1)} %param.21) | copy-start | bytes 12292
  0.0 1.8 %copy-start.11 = (bf16[64,32]{0,1:T(8,128)(2,1)S(1)}, bf16[64,32]{0,1:T(8,128)(2,1)}, u32[]{:S(2)}) copy-start(bf16[64,32]{0,1:T(8,128)(2,1)} %param.20) | copy-start | bytes 12292
  0.0 1.8 %copy-start.8 = (bf16[64,128]{1,0:T(8,128)(2,1)S(1)}, bf16[64,128]{1,0:T(8,128)(2,1)}, u32[]{:S(2)}) copy-start(bf16[64,128]{1,0:T(8,128)(2,1)} %o1.1) | copy-start | bytes 49156
  0.7 1.1 %copy-start.7 = (bf16[128,64]{0,1:T(8,128)(2,1)S(1)}, bf16[128,64]{0,1:T(8,128)(2,1)}, u32[]{:S(2)}) copy-start(bf16[128,64]{0,1:T(8,128)(2,1)} %param.29) | copy-start | bytes 49156
  1.0 0.8 copy-start.6
  1.4 0.7 copy-start.5
  1.6 0.7 copy-start.4
  1.7 0.7 copy-start.1
  1.7 0.7 copy-start.2
  1.7 0.8 copy-start.3
  2.5 1.0 %copy-start = (bf16[4096,64]{0,1:T(8,128)(2,1)S(1)}, bf16[4096,64]{0,1:T(8,128)(2,1)}, u32[]{:S(2)}) copy-start(bf16[4096,64]{0,1:T(8,128)(2,1)} %param.16) | copy-start | bytes 1572868
  44.2 1.7 %copy-start.9 = (bf16[64,128]{1,0:T(8,128)(2,1)S(1)}, bf16[64,128]{1,0:T(8,128)(2,1)}, u32[]{:S(2)}) copy-start(bf16[64,128]{1,0:T(8,128)(2,1)} %w_pool.1) | copy-start | bytes 49156
  44.2 1.7 %copy-start.10 = (bf16[128,64]{0,1:T(8,128)(2,1)S(1)}, bf16[128,64]{0,1:T(8,128)(2,1)}, u32[]{:S(2)}) copy-start(bf16[128,64]{0,1:T(8,128)(2,1)} %param.31) | copy-start | bytes 49156

commit v3 on v2

--- a/solution.py
+++ b/solution.py
@@ -14,8 +14,8 @@
 TILE = 256
 SPAN = 384
 STACK = 2
-HI_ROWS = 64
-LO_ROWS = 128
+HI_ROWS = 32
+LO_ROWS = 32
 OUTSIDE = 1 << 20
 MESH = pl.DeviceIdType.MESH
 BF16 = jnp.bfloat16
@@ -120,8 +120,9 @@
 
 def fine_kernel(ranges, window, window_marks, small, large, out, keys, values_t, queries_t, scores):
     marks = window_marks[...]
-    high = jnp.where((marks < 0) | (marks >= OUTSIDE), HI_ROWS - 1, marks // LO_ROWS)
-    low = jnp.where(marks < 0, 0, marks % LO_ROWS)
+    outside = jnp.where((marks < 0) | (marks >= OUTSIDE), 1, 0)
+    high = marks // LO_ROWS
+    low = marks % LO_ROWS
     total = window.shape[1]
     count = out.shape[1]
     width = window.shape[0]
@@ -134,7 +135,8 @@
     key_t = dot(weight[1], normed).astype(BF16)
     for start in range(0, total, TILE):
         part = slice(start, start + TILE)
-        hot_high = (lax.broadcasted_iota(jnp.int32, (HI_ROWS, TILE), 0) == high[:, part]).astype(F32)
+        code = lax.broadcasted_iota(jnp.int32, (HI_ROWS, TILE), 0)
+        hot_high = ((code == high[:, part]) | (outside[:, part] > 0)).astype(F32)
         hot_low = (lax.broadcasted_iota(jnp.int32, (LO_ROWS, TILE), 0) == low[:, part]).astype(F32)
         stacked = jnp.concatenate([key_t[:, part].astype(F32), hot_high, hot_low], axis=0)
         keys[part, :] = jnp.transpose(stacked).astype(BF16)

time: 97.6 us -> 95.5 us (0.978); the launches traced: 97.9 us -> 94.7 us
  Pallas kernels: 93.5 us -> 90.3 us
    pallas_call x6, Pallas kernels: 93.5 us -> 90.3 us  [call(): pl.pallas_call(kernel, out_shape=[jax.ShapeDtypeStruct(shape, kind) for s...]
where the time goes in v3:
time: 95.5 us; the launch traced here: 94.7 us
  Pallas kernels  90.3 us (95%)
  local copies, waits for them, and re-layouts  3.09 us (3%)
  other arithmetic  1.06 us (1%)
    pallas_call x6, Pallas kernels, call(): pl.pallas_call(kernel, out_shape=[jax.ShapeDtypeStruct(shape, kind) for s...  90.3 us
    unnamed x34, local copies, waits for them, and re-layouts  2.57 us

profile of v3, /device:TPU:0, one launch (start us, length us, event | category | flops | bytes accessed | tf_op | source)
XLA Modules:
  0.0 94.7 jit_solution(16288074069071193221)
XLA Ops:
  0.0 0.7 copy-done.15
  0.7 0.3 reduce-window.6
  1.0 0.2 slice_reduce_fusion.1
  1.2 0.2 reduce-window.9
  1.4 0.1 bitcast_add_fusion
  1.4 0.2 convert_reduce_fusion.2
  1.7 0.1 broadcast.186
  1.8 0.3 copy-done.5
  2.1 0.3 copy-done.4
  2.4 0.1 copy-done.1
  2.4 0.0 copy-done.2
  2.5 1.0 %copy-done = bf16[4096,64]{0,1:T(8,128)(2,1)S(1)} copy-done((bf16[4096,64]{0,1:T(8,128)(2,1)S(1)}, bf16[4096,64]{0,1:T(8,128)(2,1)}, u32[]{:S(2)}) %copy-start) | copy-done | bytes 524312
  3.5 9.4 %shard_map.154 = (bf16[64,4096]{1,0:T(8,128)(2,1)S(1)}, s32[1,4096]{1,0:T(1,128)S(1)}, s32[4,1,2048]{2,1,0:T(1,128)S(1)}, bf16[2,4,32,64]{3,2,1,0:T(8,128)(2,1)S(1)}, bf16[2,6,64,128]{3,2,1,0:T(8,128)(2,1)S(1)}) custom-call(bf16[64,4096]{1,0:T(8,128)(2,1)S(1)} %bitcast.41, s32[1,4096]{1,0:T(1,128)S(1)} %bitcast.45, s32[1,2048]{1,0:T(1,128)S(1)} %bitcast.43, ...), custom_call_target="tpu_custom_call" | custom-call | tf_op jit(solution)/shard_map/pallas_call | solution.py:375
  13.0 0.1 fusion.2
  13.0 0.1 copy.27
  13.1 0.1 copy.26
  13.2 0.2 convert_reduce_fusion.1
  13.5 0.1 copy.25
  13.6 0.1 reshape.194.ranges
  13.6 24.0 %shard_map.155.src = bf16[64,2048]{1,0:T(8,128)(2,1)S(1)} custom-call(s32[16]{0:T(128)S(1)} %reshape.194.ranges, bf16[64,4096]{1,0:T(8,128)(2,1)S(1)} %get-tuple-element.11.window, s32[1,4096]{1,0:T(1,128)S(1)} %and_select_fusion.1.window_marks, bf16[2,4,32,64]{3,2,1,0:T(8,128)(2,1)S(1)} %get-tuple-element.12.small, ...), custom_call_target="tpu_custom_call" | custom-call | tf_op jit(solution)/shard_map/pallas_call | solution.py:375
  37.7 8.9 %shard_map.156.fine = bf16[2,64,2048]{2,1,0:T(8,128)(2,1)S(1)} custom-call(bf16[64,2048]{1,0:T(8,128)(2,1)S(1)} %shard_map.155.src), custom_call_target="tpu_custom_call" | custom-call | tf_op jit(solution)/shard_map/pallas_call | solution.py:375
  46.6 1.7 %shard_map.157.part = bf16[64,1024]{1,0:T(8,128)(2,1)S(1)} custom-call(s32[16]{0:T(128)S(1)} %fusion.lows, bf16[2,64,2048]{2,1,0:T(8,128)(2,1)S(1)} %shard_map.156.fine, s32[1,2048]{1,0:T(1,128)S(1)} %get-tuple-element.17.starts, s32[1,2048]{1,0:T(1,128)S(1)} %get-tuple-element.18.ends), custom_call_target="tpu_custom_call" | custom-call | tf_op jit(solution)/shard_map/pallas_call | solution.py:375
  48.3 43.8 %shard_map.158.nearby = bf16[64,2048]{1,0:T(8,128)(2,1)S(1)} custom-call(bf16[64,1024]{1,0:T(8,128)(2,1)S(1)} %shard_map.157.part, s32[4,1,2048]{2,1,0:T(1,128)S(1)} %get-tuple-element.14.slots_all, s32[1,2048]{1,0:T(1,128)S(1)} %bitcast.44, bf16[2,6,64,128]{3,2,1,0:T(8,128)(2,1)S(1)} %get-tuple-element.13.large, bf16[64,128]{1,0:T(8,128)(2,1)S(1)} %copy-done.9, ...), custom_call_target="tpu_custom_call" | custom-call | tf_op jit(solution)/shard_map/pallas_call | solution.py:375
  92.2 2.5 %shard_map.159 = bf16[64,4096]{1,0:T(8,128)(2,1)} custom-call(s32[16]{0:T(128)S(1)} %fusion.lows, bf16[64,2048]{1,0:T(8,128)(2,1)S(1)} %shard_map.158.nearby, bf16[2,64,2048]{2,1,0:T(8,128)(2,1)S(1)} %shard_map.156.fine, s32[1,2048]{1,0:T(1,128)S(1)} %get-tuple-element.17.starts, s32[1,2048]{1,0:T(1,128)S(1)} %get-tuple-element.18.ends), custom_call_target="tpu_custom_call" | custom-call | tf_op jit(solution)/shard_map/pallas_call | solution.py:375
  (35 shorter events, 0.2 us)
Async XLA Ops:
  0.0 0.7 copy-start.15
  0.0 1.8 %copy-start.14 = (bf16[32,64]{1,0:T(8,128)(2,1)S(1)}, bf16[32,64]{1,0:T(8,128)(2,1)}, u32[]{:S(2)}) copy-start(bf16[32,64]{1,0:T(8,128)(2,1)} %o0.1) | copy-start | bytes 12292
  0.0 1.8 %copy-start.13 = (bf16[64,32]{0,1:T(8,128)(2,1)S(1)}, bf16[64,32]{0,1:T(8,128)(2,1)}, u32[]{:S(2)}) copy-start(bf16[64,32]{0,1:T(8,128)(2,1)} %param.22) | copy-start | bytes 12292
  0.0 1.8 %copy-start.12 = (bf16[64,32]{0,1:T(8,128)(2,1)S(1)}, bf16[64,32]{0,1:T(8,128)(2,1)}, u32[]{:S(2)}) copy-start(bf16[64,32]{0,1:T(8,128)(2,1)} %param.21) | copy-start | bytes 12292
  0.0 1.8 %copy-start.11 = (bf16[64,32]{0,1:T(8,128)(2,1)S(1)}, bf16[64,32]{0,1:T(8,128)(2,1)}, u32[]{:S(2)}) copy-start(bf16[64,32]{0,1:T(8,128)(2,1)} %param.20) | copy-start | bytes 12292
  0.0 1.8 %copy-start.8 = (bf16[64,128]{1,0:T(8,128)(2,1)S(1)}, bf16[64,128]{1,0:T(8,128)(2,1)}, u32[]{:S(2)}) copy-start(bf16[64,128]{1,0:T(8,128)(2,1)} %o1.1) | copy-start | bytes 49156
  0.7 1.1 %copy-start.7 = (bf16[128,64]{0,1:T(8,128)(2,1)S(1)}, bf16[128,64]{0,1:T(8,128)(2,1)}, u32[]{:S(2)}) copy-start(bf16[128,64]{0,1:T(8,128)(2,1)} %param.29) | copy-start | bytes 49156
  1.0 0.8 copy-start.6
  1.4 0.7 copy-start.5
  1.6 0.7 copy-start.4
  1.7 0.7 copy-start.1
  1.7 0.7 copy-start.2
  1.7 0.8 copy-start.3
  2.5 1.0 %copy-start = (bf16[4096,64]{0,1:T(8,128)(2,1)S(1)}, bf16[4096,64]{0,1:T(8,128)(2,1)}, u32[]{:S(2)}) copy-start(bf16[4096,64]{0,1:T(8,128)(2,1)} %param.16) | copy-start | bytes 1572868
  46.6 1.7 %copy-start.9 = (bf16[64,128]{1,0:T(8,128)(2,1)S(1)}, bf16[64,128]{1,0:T(8,128)(2,1)}, u32[]{:S(2)}) copy-start(bf16[64,128]{1,0:T(8,128)(2,1)} %w_pool.1) | copy-start | bytes 49156
  46.6 1.7 %copy-start.10 = (bf16[128,64]{0,1:T(8,128)(2,1)S(1)}, bf16[128,64]{0,1:T(8,128)(2,1)}, u32[]{:S(2)}) copy-start(bf16[128,64]{0,1:T(8,128)(2,1)} %param.31) | copy-start | bytes 49156
